TPU v7x, 256 devices: a whole 4x4x8 slice. The times are simulated.
256 devices in a mesh: line: 8 (over x, core), grid: 32 (over z, y).
Axes of the slice: x: 4, y: 4, z: 8, core: 2. Of those that a mesh axis runs over, the one named last changes fastest.
Arguments:
- psi_start: float32 [5, 128, 8192], P(None, 'line', 'grid'), may hold values from -6 to 6
- objective: float32 [5, 128, 8192], P(None, 'line', 'grid'), may hold values from -6 to 6
- stencil: bfloat16 [5, 5, 5, 128, 8192], P(None, None, None, 'line', 'grid'), may hold values from -0.8984375 to 0.8984375
- lower_factor: float32 [5, 5, 128, 8192], P(None, None, 'line', 'grid'), may hold values from -0.02 to 1
- upper_factor: float32 [5, 5, 128, 8192], P(None, None, 'line', 'grid'), may hold values from -0.15 to 1
- fringe_line: int32 [2048], P('grid'), may hold values from 0 to 255
- donor_owner: int32 [16384, 1], P('grid'), may hold values from 0 to 31; in each aligned block of 512 rows (0 to 511, 512 to 1023, ...) at most 32 rows name the same one
- donor_line: int32 [16384], P('grid'), may hold values from 0 to 255
- donor_weight: float32 [128, 16384], P('line', 'grid'), may hold values from 0.05 to 0.25
Outputs:
- adjoint: float32 [5, 128, 8192], P(None, 'line', 'grid')
- residual: float32 [5, 128, 8192], P(None, 'line', 'grid')
Inputs may be any that keep to these rules, and one draw needn't show every extreme that they name: `donor_owner`: in the 512 rows of each block no owner is named more than 32 times, and in some blocks one owner is named exactly 32 times.
All inputs are finite; a program needn't handle non-finite values.
Results may differ from a plain program's by a relative error of at most 0.0003.
Values sent between devices are 32-bit elements; how exact they have to be, the bound alone decides.
A program may use at most 64 MiB of HBM per device.

v0:
```python
import jax
import jax.numpy as jnp
from jax import lax
from jax.sharding import PartitionSpec as P

ITERS = 2


relaxation = 0.1


def carried_in(value, axis, join, neutral, backward):
    count, mine = (lax.axis_size(axis), lax.axis_index(axis))
    pieces = jax.tree.map(lambda part: lax.all_gather(part, axis), value)
    if backward:
        pieces = jax.tree.map(lambda part: part[::-1], pieces)
        mine = count - 1 - mine
    total = jax.tree.map(
        lambda part, zero: jnp.full_like(part, 0) + jnp.asarray(zero, part.dtype), value, neutral
    )

    def lap(position, total):
        longer = join(total, jax.tree.map(lambda part: part[position], pieces))
        return jax.tree.map(lambda new, old: jnp.where(position < mine, new, old), longer, total)

    return lax.fori_loop(0, count - 1, lap, total)


def from_behind(value, axis, steps):
    count = lax.axis_size(axis)
    leading, last = (max(0, -steps), min(count, count - steps))
    return lax.ppermute(value, axis, [(source, source + steps) for source in range(leading, last)])


def matrix_product(first_factor, second_factor):
    return jnp.sum(first_factor[:, :, None] * second_factor[None], axis=1)


def matrix_vector(matrix, vectors):
    return jnp.sum(matrix * vectors[None], axis=1)


def shift_points(values, stride, forward, filler):
    point_count = values.shape[-2]
    if forward:
        return jnp.concatenate([filler, values[..., : point_count - stride, :]], axis=-2)
    return jnp.concatenate([values[..., stride:, :], filler], axis=-2)


def build_levels(matrices, forward):
    num_vars = matrices.shape[0]
    num_points = matrices.shape[2]
    num_lines = matrices.shape[3]
    levels = []
    current = matrices
    stride = 1
    while stride < num_points:
        levels.append((stride, current))
        filler = jnp.broadcast_to(
            jnp.eye(num_vars, dtype=jnp.float32)[:, :, None, None],
            (num_vars, num_vars, stride, num_lines),
        )
        current = matrix_product(current, shift_points(current, stride, forward, filler))
        stride = stride * 2
    return (levels, current)


def local_sweep(vectors, levels, forward):
    for stride, matrix in levels:
        filler = jnp.zeros((vectors.shape[0], stride, vectors.shape[2]), jnp.float32)
        vectors = matrix_vector(matrix, shift_points(vectors, stride, forward, filler)) + vectors
    return vectors


def compose(earlier_pair, later_pair):
    joined = jnp.sum(later_pair[0][:, :, None] * earlier_pair[0][None], axis=1)
    carried = jnp.sum(later_pair[0] * earlier_pair[1][None], axis=1) + later_pair[1]
    return (joined, carried)


def chain_identity(edge_matrix):
    num_vars = edge_matrix.shape[0]
    num_lines = edge_matrix.shape[2]
    eye_blocks = jnp.broadcast_to(
        jnp.eye(num_vars, dtype=jnp.float32)[:, :, None], (num_vars, num_vars, num_lines)
    )
    return (eye_blocks, jnp.zeros((num_vars, num_lines), jnp.float32))


def apply_incoming(full_prefix, incoming):
    return jnp.sum(full_prefix * incoming[None, :, None, :], axis=1)


def chain_down(vectors, levels, full_prefix):
    partial_sums = local_sweep(vectors, levels, True)
    edge_pair = (full_prefix[:, :, -1, :], partial_sums[:, -1, :])
    incoming = carried_in(edge_pair, "line", compose, chain_identity(edge_pair[0]), False)[1]
    return apply_incoming(full_prefix, incoming) + partial_sums


def chain_up(vectors, levels, full_prefix):
    partial_sums = local_sweep(vectors, levels, False)
    edge_pair = (full_prefix[:, :, 0, :], partial_sums[:, 0, :])
    incoming = carried_in(edge_pair, "line", compose, chain_identity(edge_pair[0]), True)[1]
    return apply_incoming(full_prefix, incoming) + partial_sums


def offset_product(stencil_block, adjoint):
    return jnp.sum(stencil_block.astype(jnp.float32) * adjoint[:, None], axis=0)


def transposed_stencil(adjoint, stencil):
    product = [offset_product(stencil[offset], adjoint) for offset in range(5)]
    rim_below = from_behind(product[1][:, -1:, :], "line", 1)
    rim_above = from_behind(product[2][:, :1, :], "line", -1)
    zero_column = jnp.zeros((adjoint.shape[0], adjoint.shape[1], 1), jnp.float32)
    result = adjoint + product[0]
    result = result + jnp.concatenate([rim_below, product[1][:, :-1]], axis=1)
    result = result + jnp.concatenate([product[2][:, 1:], rim_above], axis=1)
    result = result + jnp.concatenate([zero_column, product[3][:, :, :-1]], axis=2)
    result = result + jnp.concatenate([product[4][:, :, 1:], zero_column], axis=2)
    return result


def local(
    psi_start,
    objective,
    stencil,
    lower_factor,
    upper_factor,
    fringe_line,
    donor_owner,
    donor_line,
    donor_weight,
):
    num_vars, num_points, num_lines = psi_start.shape
    row_count = donor_line.shape[0]
    down_levels, down_prefix = build_levels(lower_factor, True)
    up_levels, up_prefix = build_levels(upper_factor, False)
    owners = donor_owner[:, 0]
    source_rows = jnp.repeat(fringe_line, row_count // fringe_line.shape[0])
    target = owners * num_lines + donor_line
    adjoint = psi_start
    residual = jnp.zeros_like(psi_start)
    for iteration in range(ITERS):
        contrib = adjoint[:, :, source_rows] * donor_weight[None]
        rows_major = jnp.transpose(contrib, (2, 0, 1)).reshape(row_count, num_vars * num_points)
        count = num_lines * lax.axis_size("grid")
        local_row = target
        local_row = jnp.where((local_row >= 0) & (local_row < count), local_row, count)
        summed = lax.psum_scatter(
            jax.ops.segment_sum(rows_major, local_row, count),
            "grid",
            scatter_dimension=0,
            tiled=True,
        )
        fringe = jnp.transpose(summed.reshape(num_lines, num_vars, num_points), (1, 2, 0))
        residual = objective - transposed_stencil(adjoint, stencil) - fringe
        lowered = chain_down(residual, down_levels, down_prefix)
        update = chain_up(lowered, up_levels, up_prefix)
        adjoint = adjoint + relaxation * update
    return (adjoint, residual)


def solution(mesh):
    in_specs = (
        P(None, "line", "grid"),
        P(None, "line", "grid"),
        P(None, None, None, "line", "grid"),
        P(None, None, "line", "grid"),
        P(None, None, "line", "grid"),
        P("grid"),
        P("grid", None),
        P("grid"),
        P("line", "grid"),
    )
    out_specs = (P(None, "line", "grid"), P(None, "line", "grid"))
    return jax.shard_map(local, mesh=mesh, in_specs=in_specs, out_specs=out_specs, check_vma=False)
```

profile of v0, /device:TPU:1, one launch (start us, length us, event | category | flops | bytes accessed | tf_op | source)
XLA Modules:
  0.0 601.2 jit_solution(1863481681616915327)
XLA Ops:
  10.3 1.9 gather_fusion
  12.2 1.6 broadcast_multiply_fusion.1
  13.8 2.0 copy.287
  15.9 4.4 scatter_custom_fusion
  23.1 4.5 collective-permute-start
  28.2 2.5 collective-permute-start.1
  34.7 14.1 %all-gather.1 = f32[40,5,1,256]{3,2,1,0:T(1,128)} all-gather(f32[5,5,1,256]{3,2,1,0:T(1,128)S(1)} %slice.206), channel_id=3, replica_groups=mesh['line'=8,'grid'=32] {'line'}, dimensions={0}, use_global_device_ids=true | all-gather | bytes 230400 | tf_op jit(solution)/shard_map/all_gather | solution.py:14
  48.8 13.9 %all-gather = f32[40,5,1,256]{3,2,1,0:T(1,128)} all-gather(f32[5,5,1,256]{3,2,1,0:T(1,128)S(1)} %slice.202), channel_id=2, replica_groups=mesh['line'=8,'grid'=32] {'line'}, dimensions={0}, use_global_device_ids=true | all-gather | bytes 230400 | tf_op jit(solution)/shard_map/all_gather | solution.py:14
  63.3 1.6 slice.212
  64.9 1.7 copy.307
  66.6 1.6 copy.283
  68.2 1.7 reshape.149
  69.9 1.7 rev.10
  71.6 1.8 copy.293
  73.5 166.7 %reduce-scatter.3.cloned.1.call-done = f32[256,80]{1,0:T(8,128)} async-done(((f32[8192,80]{1,0:T(8,128)}), f32[256,80]{1,0:T(8,128)}) %reduce-scatter.3.cloned.1.call-update) | async-done | bytes 81936 | tf_op jit(solution)/shard_map/reduce_scatter | solution.py:151
  240.2 1.6 copy.289
  244.2 19.7 %all-gather.2 = f32[40,1,256]{2,1,0:T(1,128)} all-gather(f32[5,1,256]{2,1,0:T(1,128)S(1)} %slice.217), channel_id=4, replica_groups=mesh['line'=8,'grid'=32] {'line'}, dimensions={0}, use_global_device_ids=true | all-gather | bytes 46080 | tf_op jit(solution)/shard_map/all_gather | solution.py:14
  263.9 1.5 reduce
  265.4 1.4 reshape.151
  266.8 14.8 %while.56 = (s32[]{:T(128)}, f32[5,256]{1,0:T(8,128)S(1)}, s32[]{:T(128)}, f32[8,5,5,256]{3,2,1,0:T(8,128)}, f32[8,5,256]{2,1,0:T(8,128)}, /*index=5*/s32[]{:T(128)}, s32[]{:T(128)}) while((s32[]{:T(128)}, f32[5,256]{1,0:T(8,128)S(1)}, s32[]{:T(128)}, f32[8,5,5,256]{3,2,1,0:T(8,128)}, f32[8,5,256]{2,1,0:T(8,128)}, ...), condition=%wide.region_21.22_spmd.clone, body=%wide.region_19.21_spmd.clone.sunk | while | flops 16644 | bytes 66666 | solution.py:26
  266.8 1.4 fusion.41
  268.9 1.4 fusion.41
  271.0 1.4 fusion.41
  273.1 1.4 fusion.41
  275.3 1.4 fusion.41
  277.4 1.4 fusion.41
  279.5 1.4 fusion.41
  284.6 13.9 %all-gather.3 = f32[40,1,256]{2,1,0:T(1,128)} all-gather(f32[5,1,256]{2,1,0:T(1,128)S(1)} %slice.222), channel_id=5, replica_groups=mesh['line'=8,'grid'=32] {'line'}, dimensions={0}, use_global_device_ids=true | all-gather | bytes 46080 | tf_op jit(solution)/shard_map/all_gather | solution.py:14
  298.6 1.5 reduce.1
  300.0 1.4 reshape.152
  301.5 1.5 rev.11
  302.9 10.6 %while.57 = (s32[]{:T(128)}, f32[5,256]{1,0:T(8,128)S(1)}, s32[]{:T(128)}, f32[8,5,5,256]{3,2,1,0:T(8,128)}, f32[8,5,256]{2,1,0:T(8,128)}, /*index=5*/s32[]{:T(128)}, s32[]{:T(128)}) while((s32[]{:T(128)}, f32[5,256]{1,0:T(8,128)S(1)}, s32[]{:T(128)}, f32[8,5,5,256]{3,2,1,0:T(8,128)}, f32[8,5,256]{2,1,0:T(8,128)}, ...), condition=%wide.region_29.30_spmd.clone, body=%wide.region_27.29_spmd.clone.sunk | while | flops 16644 | bytes 66666 | solution.py:26
  314.6 1.6 multiply_add_fusion.1
  316.2 2.2 copy.296
  318.4 3.7 gather_fusion.1
  322.1 3.2 broadcast_multiply_fusion
  325.2 2.0 copy.297
  328.0 4.8 scatter_custom_fusion.1
  333.7 2.2 fusion.13
  336.5 2.8 collective-permute-start.2
  340.0 1.9 collective-permute-start.3
  342.5 1.6 slice.228
  344.2 202.3 %reduce-scatter.5.cloned.1.call-done = f32[256,80]{1,0:T(8,128)} async-done(((f32[8192,80]{1,0:T(8,128)}), f32[256,80]{1,0:T(8,128)}) %reduce-scatter.5.cloned.1.call-update) | async-done | bytes 81936 | tf_op jit(solution)/shard_map/reduce_scatter | solution.py:151
  546.5 1.6 copy.299
  549.7 18.4 %all-gather.4 = f32[40,1,256]{2,1,0:T(1,128)S(1)} all-gather(f32[5,1,256]{2,1,0:T(1,128)S(1)} %slice.233), channel_id=6, replica_groups=mesh['line'=8,'grid'=32] {'line'}, dimensions={0}, use_global_device_ids=true | all-gather | bytes 46080 | tf_op jit(solution)/shard_map/all_gather | solution.py:14
  568.2 6.0 while.58
  574.7 12.8 %all-gather.5 = f32[40,1,256]{2,1,0:T(1,128)S(1)} all-gather(f32[5,1,256]{2,1,0:T(1,128)S(1)} %slice.238), channel_id=7, replica_groups=mesh['line'=8,'grid'=32] {'line'}, dimensions={0}, use_global_device_ids=true | all-gather | bytes 46080 | tf_op jit(solution)/shard_map/all_gather | solution.py:14
  587.6 6.0 while.59
  (239 shorter events, 50.5 us)
Async XLA Ops:
  7.2 233.1 %reduce-scatter.3.cloned.1.call-start = ((), (), s32[]{:S(2)}) async-start(), calls=%async_computation.2 | async-start | bytes 4325376 | tf_op jit(solution)/shard_map/reduce_scatter | solution.py:151
  8.1 5.7 copy-start.13
  13.8 2.1 copy-start.16
  13.8 2.1 copy-start.14
  15.9 4.4 copy-start.15
  20.3 1.2 copy-start.2
  20.3 1.2 copy-start.8
  20.3 10.3 %copy-start.1 = (f32[5,5,16,256]{3,2,1,0:T(8,128)S(1)}, f32[5,5,16,256]{3,2,1,0:T(8,128)}, u32[]{:S(2)}) copy-start(f32[5,5,16,256]{3,2,1,0:T(8,128)} %param.21) | copy-start | bytes 1228804
  20.4 10.5 %copy-start = (f32[5,5,16,256]{3,2,1,0:T(8,128)S(1)}, f32[5,5,16,256]{3,2,1,0:T(8,128)}, u32[]{:S(2)}) copy-start(f32[5,5,16,256]{3,2,1,0:T(8,128)} %param.20) | copy-start | bytes 1228804
  20.4 526.1 %reduce-scatter.5.cloned.1.call-start = ((), (), s32[]{:S(2)}) async-start(), calls=%async_computation.3 | async-start | bytes 4325376 | tf_op jit(solution)/shard_map/reduce_scatter | solution.py:151
  22.5 8.4 %copy-start.10 = (f32[5,16,256]{2,1,0:T(8,128)}, f32[5,16,256]{2,1,0:T(8,128)S(1)}, u32[]{:S(2)}) copy-start(f32[5,16,256]{2,1,0:T(8,128)S(1)} %get-tuple-element.530) | copy-start | bytes 245764
  23.1 218.8 %collective-permute-start = (f32[5,1,256]{2,1,0:T(1,128)}, f32[5,1,256]{2,1,0:T(1,128)}, u32[]{:S(2)}, u32[]{:S(2)}) collective-permute-start(f32[5,1,256]{2,1,0:T(1,128)} %slice.207), channel_id=1, source_target_pairs={{0,32},{32,64},{64,96},{96,128},{128,160},{160,192},{192,224},{1,3... | collective-permute-start | bytes 15368 | tf_op jit(solution)/shard_map/ppermute | solution.py:32
  28.2 213.7 %collective-permute-start.1 = (f32[5,1,256]{2,1,0:T(1,128)}, f32[5,1,256]{2,1,0:T(1,128)}, u32[]{:S(2)}, u32[]{:S(2)}) collective-permute-start(f32[5,1,256]{2,1,0:T(1,128)} %slice.210), channel_id=1, source_target_pairs={{32,0},{64,32},{96,64},{128,96},{160,128},{192,160},{224,192},{33,... | collective-permute-start | bytes 15368 | tf_op jit(solution)/shard_map/ppermute | solution.py:32
  33.0 0.8 copy-start.5
  33.9 0.8 copy-start.3
  243.5 0.6 copy-start.12
  284.0 0.6 copy-start.11
  332.8 0.9 copy-start.7
  336.5 211.6 %collective-permute-start.2 = (f32[5,1,256]{2,1,0:T(1,128)}, f32[5,1,256]{2,1,0:T(1,128)S(1)}, u32[]{:S(2)}, u32[]{:S(2)}) collective-permute-start(f32[5,1,256]{2,1,0:T(1,128)} %slice.223), channel_id=1, source_target_pairs={{0,32},{32,64},{64,96},{96,128},{128,160},{160,192},{192,224},{1,3... | collective-permute-start | bytes 15368 | tf_op jit(solution)/shard_map/ppermute | solution.py:32
  340.0 208.1 %collective-permute-start.3 = (f32[5,1,256]{2,1,0:T(1,128)}, f32[5,1,256]{2,1,0:T(1,128)S(1)}, u32[]{:S(2)}, u32[]{:S(2)}) collective-permute-start(f32[5,1,256]{2,1,0:T(1,128)} %slice.226), channel_id=1, source_target_pairs={{32,0},{64,32},{96,64},{128,96},{160,128},{192,160},{224,192},{33,... | collective-permute-start | bytes 15368 | tf_op jit(solution)/shard_map/ppermute | solution.py:32
  549.3 18.9 %copy-start.9 = (f32[5,16,256]{2,1,0:T(8,128)}, f32[5,16,256]{2,1,0:T(8,128)S(1)}, u32[]{:S(2)}) copy-start(f32[5,16,256]{2,1,0:T(8,128)S(1)} %fusion.31) | copy-start | bytes 245764
  549.4 24.8 %copy-start.6 = (f32[5,5,16,256]{3,2,1,0:T(8,128)S(1)}, f32[5,5,16,256]{3,2,1,0:T(8,128)}, u32[]{:S(2)}) copy-start(f32[5,5,16,256]{3,2,1,0:T(8,128)} %copy-done.5) | copy-start | bytes 1228804
  574.4 19.3 %copy-start.4 = (f32[5,5,16,256]{3,2,1,0:T(8,128)S(1)}, f32[5,5,16,256]{3,2,1,0:T(8,128)}, u32[]{:S(2)}) copy-start(f32[5,5,16,256]{3,2,1,0:T(8,128)} %copy-done.3) | copy-start | bytes 1228804
Sparse Core Ops, SparseCore 0:
  20.5 219.6 reduce-scatter.2
  333.0 213.4 reduce-scatter.4
where the time goes:
time: 605 us; the launch traced here: 601 us
  waiting for transfers between devices  369 us (61%)
  blocking collectives  92.8 us (15%)
  other arithmetic  67.6 us (11%)
  local copies, waits for them, and re-layouts  44.3 us (7%)
  between operations  15 us (2%)
  starting transfers between devices  11.8 us (2%)
    reduce_scatter x2, waiting for transfers between devices, local(): lax.psum_scatter(jax.ops.segment_sum(rows_major, local_row, count), 'grid...  369 us
    all_gather x6, blocking collectives, carried_in(): pieces = jax.tree.map(lambda part: lax.all_gather(part, axis), value)  92.8 us
    reduce_sum x28, other arithmetic, compose(): jnp.sum(later_pair[0] * earlier_pair[1][None], axis=1) + later_pair[1]  26.6 us
  transfers between devices with their start and end apart: 6, of which 2 were waited for; matrix products, arithmetic and copies ran while one was open for 4% of the time, Pallas kernels for 0%

commit v1 on v0

v1 whole, which is shorter than its diff:
```python
import jax
import jax.numpy as jnp
from jax import lax
from jax.experimental import pallas as pl
from jax.experimental.pallas import tpu as pltpu
from jax.sharding import PartitionSpec as P

MESH = pl.DeviceIdType.MESH
ITERS = 2
NV = 5
NP = 16
NL = 256
NZ = 8
NY = 4
ND = 8
CAP = 32
ROWS = 512
FRINGE = 64
relaxation = 0.1
f32 = jnp.float32
bf16 = jnp.bfloat16
i32 = jnp.int32


def split(value):
    high = value.astype(bf16)
    low = (value - high.astype(f32)).astype(bf16)
    return high, low


def stacked(value):
    high, low = split(value)
    return jnp.concatenate([high, low], axis=0)


def iota(shape, dim):
    return lax.broadcasted_iota(i32, shape, dim)


def one_hot(mask):
    return jnp.where(mask, 1.0, 0.0).astype(bf16)


def shifted(value, stride, forward, filler):
    points = iota(value.shape, value.ndim - 2)
    if forward:
        return jnp.where(points >= stride, pltpu.roll(value, stride, value.ndim - 2), filler)
    return jnp.where(points < NP - stride, pltpu.roll(value, NP - stride, value.ndim - 2), filler)


def next_level(src, dst, stride, forward):
    @pl.loop(0, 2)
    def _(half):
        lanes = pl.ds(pl.multiple_of(half * 128, 128), 128)
        moved = [
            [shifted(src[k, j, :, lanes], stride, forward, 1.0 if k == j else 0.0) for j in range(NV)]
            for k in range(NV)
        ]
        for i in range(NV):
            row = [src[i, k, :, lanes] for k in range(NV)]
            for j in range(NV):
                total = row[0] * moved[0][j]
                for k in range(1, NV):
                    total = total + row[k] * moved[k][j]
                dst[i, j, :, lanes] = total


def sweep(vectors, levels, forward):
    for stride, matrix in levels:
        moved = [shifted(v, stride, forward, 0.0) for v in vectors]
        result = []
        for i in range(NV):
            total = vectors[i]
            for j in range(NV):
                total = total + matrix[i, j] * moved[j]
            result.append(total)
        vectors = result
    return vectors


def edge_product(block, first, vector):
    total = None
    for j in range(NV):
        term = block[(first + j) * 8 : (first + j) * 8 + 8, :] * vector[j : j + 1, :]
        total = term if total is None else total + term
    return total


def kernel(
    psi, objective, fringe_line, owner, donor_line, weight, stencil_hbm, lower_hbm, upper_hbm,
    adjoint_out, residual_out,
    stencil, lower, upper, low2, low4, low8, low_all, up2, up4, up8, up_all, up_low,
    gather_hot, mid_hot, line_hot, mid_weight,
    zsend0, zrecv0, zsend1, zrecv1, ysend, yrecv, own_sum,
    edge_mats, edges, rim_send, rim_recv, adjoint, base,
    load_sem, zs, zr, ys, yr, ls, lr, ms, mr, rs, rr,
):
    me = lax.axis_index("line")
    grid = lax.axis_index("grid")
    z = lax.div(grid, NY)
    y = lax.rem(grid, NY)

    barrier = pltpu.get_barrier_semaphore()
    z_peer = [None] + [{"grid": lax.rem(z + k, NZ) * NY + y} for k in range(1, NZ)]
    y_peer = [None] + [{"grid": z * NY + lax.rem(y + k, NY)} for k in range(1, NY)]
    l_peer = [None] + [{"line": lax.rem(me + k, ND)} for k in range(1, ND)]
    peers = z_peer[1:] + y_peer[1:] + l_peer[1:]
    for peer in peers:
        pl.semaphore_signal(barrier, inc=1, device_id=peer, device_id_type=MESH)
    loads = [
        pltpu.make_async_copy(src, dst, load_sem.at[n])
        for n, (src, dst) in enumerate([(lower_hbm, lower), (upper_hbm, upper), (stencil_hbm, stencil)])
    ]
    for load in loads:
        load.start()

    def remote(src, dst, send, recv, peer):
        return pltpu.make_async_remote_copy(
            src_ref=src, dst_ref=dst, send_sem=send, recv_sem=recv, device_id=peer, device_id_type=MESH
        )

    pending = []

    def send(copy):
        copy.start()
        pending.append(copy)

    lines = fringe_line[...]
    lines = jnp.concatenate([lines, lines + NL], axis=1)
    gather_hot[...] = one_hot(iota((2 * NL, 128), 0) == lines)

    def gathered(field):
        flat = field.reshape(NV * NP, NL)
        wide = jnp.concatenate([flat[:40], flat[40:]], axis=1)
        picked = jnp.dot(stacked(wide), gather_hot[...], preferred_element_type=f32)
        return picked[:40] + picked[40:]

    first = gathered(psi[...])
    own = owner[...]
    hot = iota((NZ * NY, ROWS), 0) == own
    before = one_hot(iota((ROWS, ROWS), 0) < iota((ROWS, ROWS), 1))
    count = jnp.dot(one_hot(hot), before, preferred_element_type=f32)
    rank = jnp.sum(jnp.where(hot, count, 0.0), axis=0, keepdims=True).astype(i32)
    own_z = own >> 2
    own_y = own & 3
    slot = own_z * 128 + ((own_y - y + own_z - z) & 3) * CAP + rank
    place = one_hot(iota((NZ * NY * CAP, ROWS), 0) == slot)
    which = iota((16, ROWS), 0)
    misc = jnp.where(
        which == 0, donor_line[...].astype(f32), jnp.where(which == 1, (iota((16, ROWS), 1) >> 3).astype(f32), 0.0)
    )
    entries = jnp.concatenate([stacked(weight[...]), misc.astype(bf16)], axis=0)
    table = lax.dot_general(entries, place, (((1,), (1,)), ((), ())), preferred_element_type=f32)
    for zt in range(NZ):
        lanes = slice(zt * 128, zt * 128 + 128)
        zsend0[zt, 0:40, :] = first
        zsend0[zt, 40:56, :] = table[0:16, lanes] + table[16:32, lanes]
        zsend0[zt, 56:64, :] = table[32:40, lanes]
    zrecv0[0] = zsend0[z]

    pl.semaphore_wait(barrier, len(peers))
    for k in (4, 3, 5, 2, 6, 1, 7):
        send(remote(zsend0.at[lax.rem(z + k, NZ)], zrecv0.at[k], zs.at[0, k], zr.at[0, k], z_peer[k]))

    loads[0].wait()
    loads[1].wait()
    next_level(lower, low2, 1, True)
    next_level(low2, low4, 2, True)
    next_level(low4, low8, 4, True)
    next_level(low8, low_all, 8, True)
    next_level(upper, up2, 1, False)
    next_level(up2, up4, 2, False)
    next_level(up4, up8, 4, False)
    next_level(up8, up_all, 8, False)
    low_levels = [(1, lower), (2, low2), (4, low4), (8, low8)]
    up_levels = [(1, upper), (2, up2), (4, up4), (8, up8)]

    @pl.loop(0, NV)
    def _(column):
        result = sweep([low_all[i, column] for i in range(NV)], up_levels, False)
        for i in range(NV):
            up_low[i, column] = result[i]

    mine = edge_mats.at[me]
    mine[...] = jnp.zeros((120, NL), f32)
    for j in range(NV):
        for i in range(NV):
            mine[j * 8 + i : j * 8 + i + 1, :] = low_all[i, j, NP - 1 : NP, :]
            mine[40 + j * 8 + i : 40 + j * 8 + i + 1, :] = up_all[i, j, 0:1, :]
            mine[80 + j * 8 + i : 80 + j * 8 + i + 1, :] = up_low[i, j, 0:1, :]
    for k in range(1, ND):
        send(remote(mine, mine, ms.at[k], mr.at[me], l_peer[k]))

    loads[2].wait()
    adjoint[...] = psi[...]

    for it in range(ITERS):
        field = [adjoint[i] for i in range(NV)]
        rim_send[it] = jnp.zeros((2, 8, NL), f32)
        points = iota((NP, NL), 0)
        across = iota((NP, NL), 1)
        for j in range(NV):
            prods = []
            for o in range(5):
                total = None
                for i in range(NV):
                    term = stencil[o, i, j].astype(f32) * field[i]
                    total = term if total is None else total + term
                prods.append(total)
            rim_send[it, 0, j : j + 1, :] = prods[1][NP - 1 : NP, :]
            rim_send[it, 1, j : j + 1, :] = prods[2][0:1, :]
            total = field[j] + prods[0]
            total = total + jnp.where(points >= 1, pltpu.roll(prods[1], 1, 0), 0.0)
            total = total + jnp.where(points < NP - 1, pltpu.roll(prods[2], NP - 1, 0), 0.0)
            total = total + jnp.where(across >= 1, pltpu.roll(prods[3], 1, 1), 0.0)
            total = total + jnp.where(across < NL - 1, pltpu.roll(prods[4], NL - 1, 1), 0.0)
            base[j] = objective[j] - total
        rims = [
            remote(rim_send.at[it, 0], rim_recv.at[it, 0], rs.at[it, 0], rr.at[it, 0], l_peer[1]),
            remote(rim_send.at[it, 1], rim_recv.at[it, 1], rs.at[it, 1], rr.at[it, 1], l_peer[ND - 1]),
        ]
        for rim in rims:
            send(rim)

        zrecv = zrecv0 if it == 0 else zrecv1
        parts = [None] * NZ
        for k in (0, 1, 7, 2, 6, 3, 5, 4):
            if k > 0:
                arrived = zrecv0.at[k] if it == 0 else zrecv1.at[k]
                remote(arrived, arrived, zs.at[it, k], zr.at[it, k], z_peer[k]).wait_recv()
            if it == 0:
                from_line = zrecv0[k, 57:58, :].astype(i32)
                from_line = jnp.concatenate([from_line, from_line + FRINGE], axis=1)
                mid_hot[k] = one_hot(iota((128, 256), 0) == from_line)
                mid_weight[k] = zrecv0[k, 40:56, :]
            picked = jnp.dot(stacked(zrecv[k, 0:40, :]), mid_hot[k], preferred_element_type=f32)
            picked = picked[:40] + picked[40:]
            picked = jnp.concatenate([picked[:, :128], picked[:, 128:]], axis=0)
            parts[k] = (picked.reshape(NV, NP, 128) * mid_weight[k][None]).reshape(NV * NP, 128)
        group = iota((1, 128), 1) >> 5

        def chosen(pick, j, half):
            value = pick(4 * half + (-j) % 4)
            for c in range(1, 4):
                value = jnp.where(group == c, pick(4 * half + (c - j) % 4), value)
            return value

        for j in (2, 1, 3, 0):
            if it == 0:
                to_line = jnp.concatenate(
                    [chosen(lambda k: zrecv0[k, 56:57, :], j, half) for half in range(2)], axis=1
                ).astype(i32)
                line_hot[j] = one_hot(iota((NL, 256), 0) == to_line)
            mixed = jnp.concatenate([chosen(lambda k: parts[k], j, half) for half in range(2)], axis=1)
            total = lax.dot_general(
                stacked(mixed), line_hot[j], (((1,), (1,)), ((), ())), preferred_element_type=f32
            )
            total = total[:80] + total[80:]
            if j == 0:
                own_sum[...] = total
            else:
                ysend[it, j - 1] = total
                send(remote(ysend.at[it, j - 1], yrecv.at[it, j - 1], ys.at[it, j], yr.at[it, j], y_peer[j]))

        for rim in rims:
            rim.wait_recv()
        below = jnp.where(me > 0, rim_recv[it, 0], 0.0)
        above = jnp.where(me < ND - 1, rim_recv[it, 1], 0.0)
        for j in range(NV):
            extra = jnp.where(points == 0, below[j : j + 1, :], 0.0)
            extra = extra + jnp.where(points == NP - 1, above[j : j + 1, :], 0.0)
            base[j] = base[j] - extra
        for j in range(1, NY):
            remote(yrecv.at[it, j - 1], yrecv.at[it, j - 1], ys.at[it, j], yr.at[it, j], y_peer[j]).wait_recv()
        fringe = (own_sum[...] + yrecv[it, 0]) + (yrecv[it, 1] + yrecv[it, 2])
        residual = base[...] - fringe.reshape(NV, NP, NL)
        if it == ITERS - 1:
            residual_out[...] = residual

        lowered = sweep([residual[i] for i in range(NV)], low_levels, True)
        raised = sweep(lowered, up_levels, False)
        edge = edges.at[it, me]
        edge[...] = jnp.zeros((16, NL), f32)
        for i in range(NV):
            edge[i : i + 1, :] = lowered[i][NP - 1 : NP, :]
            edge[8 + i : 9 + i, :] = raised[i][0:1, :]
        for k in range(1, ND):
            send(remote(edge, edge, ls.at[it, k], lr.at[it, me], l_peer[k]))
        for k in range(1, ND):
            other = lax.rem(me + k, ND)
            if it == 0:
                remote(edge_mats.at[other], edge_mats.at[other], ms.at[k], mr.at[other], l_peer[k]).wait_recv()
            remote(edges.at[it, other], edges.at[it, other], ls.at[it, k], lr.at[it, other], l_peer[k]).wait_recv()
        incoming = [jnp.zeros((8, NL), f32)]
        for f in range(ND - 1):
            incoming.append(edges[it, f, 0:8, :] + edge_product(edge_mats.at[f], 0, incoming[f]))
        returning = [jnp.zeros((8, NL), f32)] * ND
        for f in range(ND - 1, 0, -1):
            returning[f - 1] = (
                edges[it, f, 8:16, :]
                + edge_product(edge_mats.at[f], 10, incoming[f])
                + edge_product(edge_mats.at[f], 5, returning[f])
            )
        carried, back = incoming[0], returning[0]
        for f in range(1, ND):
            carried = jnp.where(me == f, incoming[f], carried)
            back = jnp.where(me == f, returning[f], back)
        for i in range(NV):
            total = raised[i]
            for j in range(NV):
                total = total + up_low[i, j] * carried[j : j + 1, :]
                total = total + up_all[i, j] * back[j : j + 1, :]
            total = adjoint[i] + relaxation * total
            adjoint[i] = total
            if it == ITERS - 1:
                adjoint_out[i] = total
        if it < ITERS - 1:
            following = gathered(adjoint[...])
            zsend1[...] = following
            zrecv1[0] = following
            for k in (4, 3, 5, 2, 6, 1, 7):
                send(remote(zsend1, zrecv1.at[k], zs.at[1, k], zr.at[1, k], z_peer[k]))

    for copy in pending:
        copy.wait_send()


def local(psi, objective, stencil, lower, upper, fringe_line, owner, donor_line, weight):
    vmem = pl.BlockSpec(memory_space=pltpu.VMEM)
    hbm = pl.BlockSpec(memory_space=pl.ANY)
    field = jax.ShapeDtypeStruct((NV, NP, NL), f32)
    matrix = pltpu.VMEM((NV, NV, NP, NL), f32)
    dma = pltpu.SemaphoreType.DMA
    return pl.pallas_call(
        kernel,
        out_shape=(field, field),
        in_specs=[vmem] * 6 + [hbm] * 3,
        out_specs=(vmem, vmem),
        scratch_shapes=[
            pltpu.VMEM((5, NV, NV, NP, NL), bf16),
            *[matrix] * 11,
            pltpu.VMEM((2 * NL, 128), bf16),
            pltpu.VMEM((NZ, 128, 256), bf16),
            pltpu.VMEM((NY, NL, 256), bf16),
            pltpu.VMEM((NZ, NP, 128), f32),
            pltpu.VMEM((NZ, 64, 128), f32),
            pltpu.VMEM((NZ, 64, 128), f32),
            pltpu.VMEM((40, 128), f32),
            pltpu.VMEM((NZ, 40, 128), f32),
            pltpu.VMEM((ITERS, NY - 1, NV * NP, NL), f32),
            pltpu.VMEM((ITERS, NY - 1, NV * NP, NL), f32),
            pltpu.VMEM((NV * NP, NL), f32),
            pltpu.VMEM((ND, 120, NL), f32),
            pltpu.VMEM((ITERS, ND, 16, NL), f32),
            pltpu.VMEM((ITERS, 2, 8, NL), f32),
            pltpu.VMEM((ITERS, 2, 8, NL), f32),
            pltpu.VMEM((NV, NP, NL), f32),
            pltpu.VMEM((NV, NP, NL), f32),
            dma((3,)),
            dma((ITERS, NZ)), dma((ITERS, NZ)),
            dma((ITERS, NY)), dma((ITERS, NY)),
            dma((ITERS, ND)), dma((ITERS, ND)),
            dma((ND,)), dma((ND,)),
            dma((ITERS, 2)), dma((ITERS, 2)),
        ],
        compiler_params=pltpu.CompilerParams(
            collective_id=0, has_side_effects=True, vmem_limit_bytes=56 * 2**20
        ),
        cost_estimate=pl.CostEstimate(flops=20_000_000, bytes_accessed=4_000_000, transcendentals=0),
        name="smooth",
    )(
        psi, objective, fringe_line.reshape(1, FRINGE), owner.reshape(1, ROWS), donor_line.reshape(1, ROWS), weight,
        stencil, lower, upper,
    )


def solution(mesh):
    in_specs = (
        P(None, "line", "grid"),
        P(None, "line", "grid"),
        P(None, None, None, "line", "grid"),
        P(None, None, "line", "grid"),
        P(None, None, "line", "grid"),
        P("grid"),
        P("grid", None),
        P("grid"),
        P("line", "grid"),
    )
    out_specs = (P(None, "line", "grid"), P(None, "line", "grid"))
    return jax.shard_map(local, mesh=mesh, in_specs=in_specs, out_specs=out_specs, check_vma=False)
```

time: 605 us -> 51.4 us (0.08)
  waiting for transfers between devices: 369 us -> 0 us
  blocking collectives: 92.8 us -> 0 us
  other arithmetic: 67.6 us -> 0 us
  Pallas kernels: 0 us -> 48.4 us
  local copies, waits for them, and re-layouts: 44.3 us -> 2.2 us
  between operations: 15 us -> 0.65 us
  starting transfers between devices: 11.8 us -> 0 us
    reduce_scatter x2 -> x0, waiting for transfers between devices: 369 us -> none  [local(): lax.psum_scatter(jax.ops.segment_sum(rows_major, local_row, count), 'grid...]
    all_gather x6 -> x0, blocking collectives: 92.8 us -> none  [carried_in(): pieces = jax.tree.map(lambda part: lax.all_gather(part, axis), value)]
    pallas_call x0 -> x1, Pallas kernels: none -> 48.4 us  [local(): pl.pallas_call(kernel, out_shape=(field, field), in_specs=[vmem] * 6 + [h...]
    reduce_sum x57 -> x0, other arithmetic: 33.9 us -> none  [the longest x28 26.6 us: compose(): jnp.sum(later_pair[0] * earlier_pair[1][None], axis=1) + later_pair[1]]
    ppermute x4 -> x0, starting transfers between devices: 11.7 us -> none  [from_behind(): lax.ppermute(value, axis, [(source, source + steps) for source in range(l...]
    select_n x30 -> x0, other arithmetic: 10.1 us -> none  [the longest x28 10.1 us: lap(): jnp.where(position < mine, new, old)]
    scatter-add x2 -> x0, other arithmetic: 9.17 us -> none  [local(): jax.ops.segment_sum(rows_major, local_row, count)]
    unnamed x37 -> x4, local copies, waits for them, and re-layouts: 9.61 us -> 2.2 us
  transfers between devices with their start and end apart: 6 -> 0, of which waited for: 2 -> 0; matrix products, arithmetic and copies ran while one was open for 4% -> 0% of each run, Pallas kernels for 0% -> 0%
where the time goes in v1:
time: 51.4 us; the launch traced here: 51.3 us
  Pallas kernels  48.4 us (94%)
  local copies, waits for them, and re-layouts  2.2 us (4%)
  between operations  0.65 us (1%)
    pallas_call x1, Pallas kernels, local(): pl.pallas_call(kernel, out_shape=(field, field), in_specs=[vmem] * 6 + [h...  48.4 us
    unnamed x4, local copies, waits for them, and re-layouts  2.2 us

profile of v1, /device:TPU:1, one launch (start us, length us, event | category | flops | bytes accessed | tf_op | source)
XLA Modules:
  0.0 51.3 jit_solution(6614916406661639381)
XLA Ops:
  0.6 48.4 %smooth.1 = (f32[5,16,256]{2,1,0:T(8,128)}, f32[5,16,256]{2,1,0:T(8,128)}) custom-call(f32[5,16,256]{2,1,0:T(8,128)} %psi.1, f32[5,16,256]{2,1,0:T(8,128)} %objective.1, s32[1,64]{1,0:T(1,128)} %bitcast.5, s32[1,512]{1,0:T(1,128)} %bitcast.3, s32[1,512]{1,0:T(1,128)} %bitcast.4, f32[16,512]{1,0:T(8,128)} %weight.1, bf16[5,5,5,16,256]{4,3,2,1,0:T(8,128)(2,1)} %stencil_hbm.1, ...), custom_call_target="tpu_custom_call" | custom-call | flops 20000000 | bytes 4000000 | tf_op jit(solution)/shard_map/smooth/pallas_call | solution.py:334
  49.1 0.0 copy-start
  49.1 1.6 %copy.13 = f32[5,16,256]{2,1,0:T(8,128)} copy(f32[5,16,256]{2,1,0:T(8,128)} %get-tuple-element.4) | data formatting | bytes 163840
  50.6 0.0 copy-done
  50.7 0.6 %copy.14 = f32[5,16,256]{2,1,0:T(8,128)} copy(f32[5,16,256]{2,1,0:T(8,128)S(1)} %copy-done) | data formatting | bytes 163840
Async XLA Ops:
  49.1 1.6 %copy-start = (f32[5,16,256]{2,1,0:T(8,128)S(1)}, f32[5,16,256]{2,1,0:T(8,128)}, u32[]{:S(2)}) copy-start(f32[5,16,256]{2,1,0:T(8,128)} %get-tuple-element.5) | copy-start | bytes 245764

commit v2 on v1

--- a/solution.py
+++ b/solution.py
@@ -87,9 +87,9 @@
 
 
 def kernel(
-    psi, objective, fringe_line, owner, donor_line, weight, stencil_hbm, lower_hbm, upper_hbm,
+    psi_hbm, objective_hbm, fringe_line_hbm, owner_hbm, donor_line_hbm, weight_hbm, stencil_hbm, lower_hbm, upper_hbm,
     adjoint_out, residual_out,
-    stencil, lower, upper, low2, low4, low8, low_all, up2, up4, up8, up_all, up_low,
+    psi, objective, fringe_line, owner, donor_line, weight, stencil, lower, upper, low2, low4, low8, low_all, up2, up4, up8, up_all, up_low,
     gather_hot, mid_hot, line_hot, mid_weight,
     zsend0, zrecv0, zsend1, zrecv1, ysend, yrecv, own_sum,
     edge_mats, edges, rim_send, rim_recv, adjoint, base,
@@ -109,7 +109,11 @@
         pl.semaphore_signal(barrier, inc=1, device_id=peer, device_id_type=MESH)
     loads = [
         pltpu.make_async_copy(src, dst, load_sem.at[n])
-        for n, (src, dst) in enumerate([(lower_hbm, lower), (upper_hbm, upper), (stencil_hbm, stencil)])
+        for n, (src, dst) in enumerate([
+            (fringe_line_hbm, fringe_line), (psi_hbm, psi), (owner_hbm, owner), (donor_line_hbm, donor_line),
+            (weight_hbm, weight), (lower_hbm, lower), (upper_hbm, upper), (stencil_hbm, stencil),
+            (objective_hbm, objective),
+        ])
     ]
     for load in loads:
         load.start()
@@ -125,6 +129,8 @@
         copy.start()
         pending.append(copy)
 
+    loads[0].wait()
+    loads[1].wait()
     lines = fringe_line[...]
     lines = jnp.concatenate([lines, lines + NL], axis=1)
     gather_hot[...] = one_hot(iota((2 * NL, 128), 0) == lines)
@@ -136,6 +142,8 @@
         return picked[:40] + picked[40:]
 
     first = gathered(psi[...])
+    for load in loads[2:5]:
+        load.wait()
     own = owner[...]
     hot = iota((NZ * NY, ROWS), 0) == own
     before = one_hot(iota((ROWS, ROWS), 0) < iota((ROWS, ROWS), 1))
@@ -155,15 +163,15 @@
         lanes = slice(zt * 128, zt * 128 + 128)
         zsend0[zt, 0:40, :] = first
         zsend0[zt, 40:56, :] = table[0:16, lanes] + table[16:32, lanes]
-        zsend0[zt, 56:64, :] = table[32:40, lanes]
+        zsend0[zt, 56:58, :] = table[32:34, lanes]
     zrecv0[0] = zsend0[z]
 
     pl.semaphore_wait(barrier, len(peers))
     for k in (4, 3, 5, 2, 6, 1, 7):
         send(remote(zsend0.at[lax.rem(z + k, NZ)], zrecv0.at[k], zs.at[0, k], zr.at[0, k], z_peer[k]))
 
-    loads[0].wait()
-    loads[1].wait()
+    loads[5].wait()
+    loads[6].wait()
     next_level(lower, low2, 1, True)
     next_level(low2, low4, 2, True)
     next_level(low4, low8, 4, True)
@@ -191,7 +199,8 @@
     for k in range(1, ND):
         send(remote(mine, mine, ms.at[k], mr.at[me], l_peer[k]))
 
-    loads[2].wait()
+    loads[7].wait()
+    loads[8].wait()
     adjoint[...] = psi[...]
 
     for it in range(ITERS):
@@ -328,23 +337,29 @@
 def local(psi, objective, stencil, lower, upper, fringe_line, owner, donor_line, weight):
     vmem = pl.BlockSpec(memory_space=pltpu.VMEM)
     hbm = pl.BlockSpec(memory_space=pl.ANY)
-    field = jax.ShapeDtypeStruct((NV, NP, NL), f32)
+    field = pltpu.VMEM((NV, NP, NL), f32)
     matrix = pltpu.VMEM((NV, NV, NP, NL), f32)
     dma = pltpu.SemaphoreType.DMA
     return pl.pallas_call(
         kernel,
         out_shape=(field, field),
-        in_specs=[vmem] * 6 + [hbm] * 3,
+        in_specs=[hbm] * 9,
         out_specs=(vmem, vmem),
         scratch_shapes=[
+            pltpu.VMEM((NV, NP, NL), f32),
+            pltpu.VMEM((NV, NP, NL), f32),
+            pltpu.VMEM((1, FRINGE), i32),
+            pltpu.VMEM((1, ROWS), i32),
+            pltpu.VMEM((1, ROWS), i32),
+            pltpu.VMEM((NP, ROWS), f32),
             pltpu.VMEM((5, NV, NV, NP, NL), bf16),
             *[matrix] * 11,
             pltpu.VMEM((2 * NL, 128), bf16),
             pltpu.VMEM((NZ, 128, 256), bf16),
             pltpu.VMEM((NY, NL, 256), bf16),
             pltpu.VMEM((NZ, NP, 128), f32),
-            pltpu.VMEM((NZ, 64, 128), f32),
-            pltpu.VMEM((NZ, 64, 128), f32),
+            pltpu.VMEM((NZ, 58, 128), f32),
+            pltpu.VMEM((NZ, 58, 128), f32),
             pltpu.VMEM((40, 128), f32),
             pltpu.VMEM((NZ, 40, 128), f32),
             pltpu.VMEM((ITERS, NY - 1, NV * NP, NL), f32),
@@ -356,7 +371,7 @@
             pltpu.VMEM((ITERS, 2, 8, NL), f32),
             pltpu.VMEM((NV, NP, NL), f32),
             pltpu.VMEM((NV, NP, NL), f32),
-            dma((3,)),
+            dma((9,)),
             dma((ITERS, NZ)), dma((ITERS, NZ)),
             dma((ITERS, NY)), dma((ITERS, NY)),
             dma((ITERS, ND)), dma((ITERS, ND)),

time: 51.4 us -> 48.1 us (0.936)
  Pallas kernels: 48.4 us -> 46.1 us
  local copies, waits for them, and re-layouts: 2.2 us -> 1.27 us
    pallas_call x1, Pallas kernels: 48.4 us -> 46.1 us  [local(): pl.pallas_call(kernel, out_shape=(field, field), in_specs=[hbm] * 9, out_...]
    unnamed x4 -> x2, local copies, waits for them, and re-layouts: 2.2 us -> 1.27 us
where the time goes in v2:
time: 48.1 us; the launch traced here: 48 us
  Pallas kernels  46.1 us (96%)
  local copies, waits for them, and re-layouts  1.27 us (3%)
  between operations  0.64 us (1%)
    pallas_call x1, Pallas kernels, local(): pl.pallas_call(kernel, out_shape=(field, field), in_specs=[hbm] * 9, out_...  46.1 us
    unnamed x2, local copies, waits for them, and re-layouts  1.27 us

profile of v2, /device:TPU:1, one launch (start us, length us, event | category | flops | bytes accessed | tf_op | source)
XLA Modules:
  0.0 48.0 jit_solution(9808559523340598488)
XLA Ops:
  0.6 46.1 %smooth.1 = (f32[5,16,256]{2,1,0:T(8,128)S(1)}, f32[5,16,256]{2,1,0:T(8,128)S(1)}) custom-call(f32[5,16,256]{2,1,0:T(8,128)} %psi_hbm.1, f32[5,16,256]{2,1,0:T(8,128)} %objective_hbm.1, s32[1,64]{1,0:T(1,128)} %bitcast.5, s32[1,512]{1,0:T(1,128)} %bitcast.3, s32[1,512]{1,0:T(1,128)} %bitcast.4, f32[16,512]{1,0:T(8,128)} %weight_hbm.1, ...), custom_call_target="tpu_custom_call" | custom-call | flops 20000000 | bytes 4000000 | tf_op jit(solution)/shard_map/smooth/pallas_call | solution.py:343
  46.7 0.6 %copy.13 = f32[5,16,256]{2,1,0:T(8,128)} copy(f32[5,16,256]{2,1,0:T(8,128)S(1)} %get-tuple-element.2) | data formatting | bytes 163840
  47.4 0.6 %copy.14 = f32[5,16,256]{2,1,0:T(8,128)} copy(f32[5,16,256]{2,1,0:T(8,128)S(1)} %get-tuple-element.3) | data formatting | bytes 163840

commit v3 on v2

--- a/solution.py
+++ b/solution.py
@@ -81,19 +81,19 @@
 def edge_product(block, first, vector):
     total = None
     for j in range(NV):
-        term = block[(first + j) * 8 : (first + j) * 8 + 8, :] * vector[j : j + 1, :]
+        term = block[first + j] * vector[j : j + 1, :]
         total = term if total is None else total + term
     return total
 
 
 def kernel(
     psi_hbm, objective_hbm, fringe_line_hbm, owner_hbm, donor_line_hbm, weight_hbm, stencil_hbm, lower_hbm, upper_hbm,
-    adjoint_out, residual_out,
+    both_out,
     psi, objective, fringe_line, owner, donor_line, weight, stencil, lower, upper, low2, low4, low8, low_all, up2, up4, up8, up_all, up_low,
-    gather_hot, mid_hot, line_hot, mid_weight,
-    zsend0, zrecv0, zsend1, zrecv1, ysend, yrecv, own_sum,
+    gather_hot, mid_hot, line_hot,
+    tab_send, tab_recv, zsend, zrecv, ysend, yrecv, own_sum,
     edge_mats, edges, rim_send, rim_recv, adjoint, base,
-    load_sem, zs, zr, ys, yr, ls, lr, ms, mr, rs, rr,
+    load_sem, ts, tr, zs, zr, ys, yr, ls, lr, ms, mr, rs, rr,
 ):
     me = lax.axis_index("line")
     grid = lax.axis_index("grid")
@@ -161,53 +161,21 @@
     table = lax.dot_general(entries, place, (((1,), (1,)), ((), ())), preferred_element_type=f32)
     for zt in range(NZ):
         lanes = slice(zt * 128, zt * 128 + 128)
-        zsend0[zt, 0:40, :] = first
-        zsend0[zt, 40:56, :] = table[0:16, lanes] + table[16:32, lanes]
-        zsend0[zt, 56:58, :] = table[32:34, lanes]
-    zrecv0[0] = zsend0[z]
-
-    pl.semaphore_wait(barrier, len(peers))
-    for k in (4, 3, 5, 2, 6, 1, 7):
-        send(remote(zsend0.at[lax.rem(z + k, NZ)], zrecv0.at[k], zs.at[0, k], zr.at[0, k], z_peer[k]))
-
-    loads[5].wait()
-    loads[6].wait()
-    next_level(lower, low2, 1, True)
-    next_level(low2, low4, 2, True)
-    next_level(low4, low8, 4, True)
-    next_level(low8, low_all, 8, True)
-    next_level(upper, up2, 1, False)
-    next_level(up2, up4, 2, False)
-    next_level(up4, up8, 4, False)
-    next_level(up8, up_all, 8, False)
-    low_levels = [(1, lower), (2, low2), (4, low4), (8, low8)]
-    up_levels = [(1, upper), (2, up2), (4, up4), (8, up8)]
-
-    @pl.loop(0, NV)
-    def _(column):
-        result = sweep([low_all[i, column] for i in range(NV)], up_levels, False)
-        for i in range(NV):
-            up_low[i, column] = result[i]
-
-    mine = edge_mats.at[me]
-    mine[...] = jnp.zeros((120, NL), f32)
-    for j in range(NV):
-        for i in range(NV):
-            mine[j * 8 + i : j * 8 + i + 1, :] = low_all[i, j, NP - 1 : NP, :]
-            mine[40 + j * 8 + i : 40 + j * 8 + i + 1, :] = up_all[i, j, 0:1, :]
-            mine[80 + j * 8 + i : 80 + j * 8 + i + 1, :] = up_low[i, j, 0:1, :]
-    for k in range(1, ND):
-        send(remote(mine, mine, ms.at[k], mr.at[me], l_peer[k]))
+        tab_send[zt, 0:16, :] = table[0:16, lanes] + table[16:32, lanes]
+        tab_send[zt, 16:18, :] = table[32:34, lanes]
+    tab_recv[0] = tab_send[z]
+    zsend[0] = first
+    zrecv[0, 0] = first
 
     loads[7].wait()
     loads[8].wait()
     adjoint[...] = psi[...]
 
-    for it in range(ITERS):
+    points = iota((NP, NL), 0)
+    across = iota((NP, NL), 1)
+
+    def local_part(it):
         field = [adjoint[i] for i in range(NV)]
-        rim_send[it] = jnp.zeros((2, 8, NL), f32)
-        points = iota((NP, NL), 0)
-        across = iota((NP, NL), 1)
         for j in range(NV):
             prods = []
             for o in range(5):
@@ -224,28 +192,56 @@
             total = total + jnp.where(across >= 1, pltpu.roll(prods[3], 1, 1), 0.0)
             total = total + jnp.where(across < NL - 1, pltpu.roll(prods[4], NL - 1, 1), 0.0)
             base[j] = objective[j] - total
+
+    def start_rims(it):
         rims = [
             remote(rim_send.at[it, 0], rim_recv.at[it, 0], rs.at[it, 0], rr.at[it, 0], l_peer[1]),
             remote(rim_send.at[it, 1], rim_recv.at[it, 1], rs.at[it, 1], rr.at[it, 1], l_peer[ND - 1]),
         ]
         for rim in rims:
             send(rim)
-
-        zrecv = zrecv0 if it == 0 else zrecv1
-        parts = [None] * NZ
-        for k in (0, 1, 7, 2, 6, 3, 5, 4):
-            if k > 0:
-                arrived = zrecv0.at[k] if it == 0 else zrecv1.at[k]
-                remote(arrived, arrived, zs.at[it, k], zr.at[it, k], z_peer[k]).wait_recv()
-            if it == 0:
-                from_line = zrecv0[k, 57:58, :].astype(i32)
-                from_line = jnp.concatenate([from_line, from_line + FRINGE], axis=1)
-                mid_hot[k] = one_hot(iota((128, 256), 0) == from_line)
-                mid_weight[k] = zrecv0[k, 40:56, :]
-            picked = jnp.dot(stacked(zrecv[k, 0:40, :]), mid_hot[k], preferred_element_type=f32)
-            picked = picked[:40] + picked[40:]
-            picked = jnp.concatenate([picked[:, :128], picked[:, 128:]], axis=0)
-            parts[k] = (picked.reshape(NV, NP, 128) * mid_weight[k][None]).reshape(NV * NP, 128)
+        return rims
+
+    local_part(0)
+    pl.semaphore_wait(barrier, len(peers))
+    for k in (4, 3, 5, 2, 6, 1, 7):
+        send(remote(tab_send.at[lax.rem(z + k, NZ)], tab_recv.at[k], ts.at[k], tr.at[k], z_peer[k]))
+    for k in (4, 3, 5, 2, 6, 1, 7):
+        send(remote(zsend.at[0], zrecv.at[0, k], zs.at[0, k], zr.at[0, k], z_peer[k]))
+
+    rims = start_rims(0)
+    loads[5].wait()
+    loads[6].wait()
+    next_level(lower, low2, 1, True)
+    next_level(low2, low4, 2, True)
+    next_level(low4, low8, 4, True)
+    next_level(low8, low_all, 8, True)
+    next_level(upper, up2, 1, False)
+    next_level(up2, up4, 2, False)
+    next_level(up4, up8, 4, False)
+    next_level(up8, up_all, 8, False)
+    low_levels = [(1, lower), (2, low2), (4, low4), (8, low8)]
+    up_levels = [(1, upper), (2, up2), (4, up4), (8, up8)]
+
+    @pl.loop(0, NV)
+    def _(column):
+        result = sweep([low_all[i, column] for i in range(NV)], up_levels, False)
+        for i in range(NV):
+            up_low[i, column] = result[i]
+
+    mine = edge_mats.at[me]
+    for j in range(NV):
+        for i in range(NV):
+            mine[j, i : i + 1, :] = low_all[i, j, NP - 1 : NP, :]
+            mine[5 + j, i : i + 1, :] = up_all[i, j, 0:1, :]
+            mine[10 + j, i : i + 1, :] = up_low[i, j, 0:1, :]
+    for k in range(1, ND):
+        send(remote(mine, mine, ms.at[k], mr.at[me], l_peer[k]))
+
+    for it in range(ITERS):
+        if it > 0:
+            local_part(it)
+            rims = start_rims(it)
         group = iota((1, 128), 1) >> 5
 
         def chosen(pick, j, half):
@@ -254,12 +250,31 @@
                 value = jnp.where(group == c, pick(4 * half + (c - j) % 4), value)
             return value
 
-        for j in (2, 1, 3, 0):
-            if it == 0:
+        if it == 0:
+            for k in range(1, NZ):
+                remote(tab_recv.at[k], tab_recv.at[k], ts.at[k], tr.at[k], z_peer[k]).wait_recv()
+            for k in range(NZ):
+                from_line = tab_recv[k, 17:18, :].astype(i32)
+                from_line = jnp.concatenate([from_line, from_line + FRINGE], axis=1)
+                picks = one_hot(iota((128, 256), 0) == from_line)
+                mid_hot[k, 0:128, :] = picks
+                mid_hot[k, 128:256, :] = picks
+            for j in range(NY):
                 to_line = jnp.concatenate(
-                    [chosen(lambda k: zrecv0[k, 56:57, :], j, half) for half in range(2)], axis=1
+                    [chosen(lambda k: tab_recv[k, 16:17, :], j, half) for half in range(2)], axis=1
                 ).astype(i32)
                 line_hot[j] = one_hot(iota((NL, 256), 0) == to_line)
+        parts = [None] * NZ
+        for k in range(1, NZ):
+            remote(zrecv.at[it, k], zrecv.at[it, k], zs.at[it, k], zr.at[it, k], z_peer[k]).wait_recv()
+        for k in range(NZ):
+            picked = jnp.dot(
+                jnp.concatenate(split(zrecv[it, k]), axis=1), mid_hot[k], preferred_element_type=f32
+            )
+            picked = jnp.concatenate([picked[:, :128], picked[:, 128:]], axis=0)
+            parts[k] = (picked.reshape(NV, NP, 128) * tab_recv[k, 0:16, :][None]).reshape(NV * NP, 128)
+
+        for j in (2, 1, 3, 0):
             mixed = jnp.concatenate([chosen(lambda k: parts[k], j, half) for half in range(2)], axis=1)
             total = lax.dot_general(
                 stacked(mixed), line_hot[j], (((1,), (1,)), ((), ())), preferred_element_type=f32
@@ -279,20 +294,21 @@
             extra = jnp.where(points == 0, below[j : j + 1, :], 0.0)
             extra = extra + jnp.where(points == NP - 1, above[j : j + 1, :], 0.0)
             base[j] = base[j] - extra
-        for j in range(1, NY):
+        for j in (3, 1, 2):
             remote(yrecv.at[it, j - 1], yrecv.at[it, j - 1], ys.at[it, j], yr.at[it, j], y_peer[j]).wait_recv()
-        fringe = (own_sum[...] + yrecv[it, 0]) + (yrecv[it, 1] + yrecv[it, 2])
-        residual = base[...] - fringe.reshape(NV, NP, NL)
+            if j == 1:
+                fringe = own_sum[...] + (yrecv[it, 0] + yrecv[it, 2])
+                base[...] = base[...] - fringe.reshape(NV, NP, NL)
+        residual = base[...] - yrecv[it, 1].reshape(NV, NP, NL)
         if it == ITERS - 1:
-            residual_out[...] = residual
+            both_out[1] = residual
 
         lowered = sweep([residual[i] for i in range(NV)], low_levels, True)
         raised = sweep(lowered, up_levels, False)
         edge = edges.at[it, me]
-        edge[...] = jnp.zeros((16, NL), f32)
-        for i in range(NV):
-            edge[i : i + 1, :] = lowered[i][NP - 1 : NP, :]
-            edge[8 + i : 9 + i, :] = raised[i][0:1, :]
+        for i in range(NV):
+            edge[0, i : i + 1, :] = lowered[i][NP - 1 : NP, :]
+            edge[1, i : i + 1, :] = raised[i][0:1, :]
         for k in range(1, ND):
             send(remote(edge, edge, ls.at[it, k], lr.at[it, me], l_peer[k]))
         for k in range(1, ND):
@@ -300,13 +316,13 @@
             if it == 0:
                 remote(edge_mats.at[other], edge_mats.at[other], ms.at[k], mr.at[other], l_peer[k]).wait_recv()
             remote(edges.at[it, other], edges.at[it, other], ls.at[it, k], lr.at[it, other], l_peer[k]).wait_recv()
-        incoming = [jnp.zeros((8, NL), f32)]
+        incoming = [jnp.zeros((NV, NL), f32)]
         for f in range(ND - 1):
-            incoming.append(edges[it, f, 0:8, :] + edge_product(edge_mats.at[f], 0, incoming[f]))
-        returning = [jnp.zeros((8, NL), f32)] * ND
+            incoming.append(edges[it, f, 0] + edge_product(edge_mats.at[f], 0, incoming[f]))
+        returning = [jnp.zeros((NV, NL), f32)] * ND
         for f in range(ND - 1, 0, -1):
             returning[f - 1] = (
-                edges[it, f, 8:16, :]
+                edges[it, f, 1]
                 + edge_product(edge_mats.at[f], 10, incoming[f])
                 + edge_product(edge_mats.at[f], 5, returning[f])
             )
@@ -322,13 +338,13 @@
             total = adjoint[i] + relaxation * total
             adjoint[i] = total
             if it == ITERS - 1:
-                adjoint_out[i] = total
+                both_out[0, i] = total
         if it < ITERS - 1:
             following = gathered(adjoint[...])
-            zsend1[...] = following
-            zrecv1[0] = following
+            zsend[1] = following
+            zrecv[1, 0] = following
             for k in (4, 3, 5, 2, 6, 1, 7):
-                send(remote(zsend1, zrecv1.at[k], zs.at[1, k], zr.at[1, k], z_peer[k]))
+                send(remote(zsend.at[1], zrecv.at[1, k], zs.at[1, k], zr.at[1, k], z_peer[k]))
 
     for copy in pending:
         copy.wait_send()
@@ -337,14 +353,14 @@
 def local(psi, objective, stencil, lower, upper, fringe_line, owner, donor_line, weight):
     vmem = pl.BlockSpec(memory_space=pltpu.VMEM)
     hbm = pl.BlockSpec(memory_space=pl.ANY)
-    field = pltpu.VMEM((NV, NP, NL), f32)
+    field = pltpu.VMEM((2, NV, NP, NL), f32)
     matrix = pltpu.VMEM((NV, NV, NP, NL), f32)
     dma = pltpu.SemaphoreType.DMA
-    return pl.pallas_call(
+    both = pl.pallas_call(
         kernel,
-        out_shape=(field, field),
+        out_shape=field,
         in_specs=[hbm] * 9,
-        out_specs=(vmem, vmem),
+        out_specs=vmem,
         scratch_shapes=[
             pltpu.VMEM((NV, NP, NL), f32),
             pltpu.VMEM((NV, NP, NL), f32),
@@ -355,23 +371,23 @@
             pltpu.VMEM((5, NV, NV, NP, NL), bf16),
             *[matrix] * 11,
             pltpu.VMEM((2 * NL, 128), bf16),
-            pltpu.VMEM((NZ, 128, 256), bf16),
+            pltpu.VMEM((NZ, 256, 256), bf16),
             pltpu.VMEM((NY, NL, 256), bf16),
-            pltpu.VMEM((NZ, NP, 128), f32),
-            pltpu.VMEM((NZ, 58, 128), f32),
-            pltpu.VMEM((NZ, 58, 128), f32),
-            pltpu.VMEM((40, 128), f32),
-            pltpu.VMEM((NZ, 40, 128), f32),
+            pltpu.VMEM((NZ, 18, 128), f32),
+            pltpu.VMEM((NZ, 18, 128), f32),
+            pltpu.VMEM((ITERS, 40, 128), f32),
+            pltpu.VMEM((ITERS, NZ, 40, 128), f32),
             pltpu.VMEM((ITERS, NY - 1, NV * NP, NL), f32),
             pltpu.VMEM((ITERS, NY - 1, NV * NP, NL), f32),
             pltpu.VMEM((NV * NP, NL), f32),
-            pltpu.VMEM((ND, 120, NL), f32),
-            pltpu.VMEM((ITERS, ND, 16, NL), f32),
-            pltpu.VMEM((ITERS, 2, 8, NL), f32),
-            pltpu.VMEM((ITERS, 2, 8, NL), f32),
+            pltpu.VMEM((ND, 15, NV, NL), f32),
+            pltpu.VMEM((ITERS, ND, 2, NV, NL), f32),
+            pltpu.VMEM((ITERS, 2, NV, NL), f32),
+            pltpu.VMEM((ITERS, 2, NV, NL), f32),
             pltpu.VMEM((NV, NP, NL), f32),
             pltpu.VMEM((NV, NP, NL), f32),
             dma((9,)),
+            dma((NZ,)), dma((NZ,)),
             dma((ITERS, NZ)), dma((ITERS, NZ)),
             dma((ITERS, NY)), dma((ITERS, NY)),
             dma((ITERS, ND)), dma((ITERS, ND)),
@@ -387,6 +403,7 @@
         psi, objective, fringe_line.reshape(1, FRINGE), owner.reshape(1, ROWS), donor_line.reshape(1, ROWS), weight,
         stencil, lower, upper,
     )
+    return both[0], both[1]
 
 
 def solution(mesh):

time: 48.1 us -> 45.6 us (0.948)
  Pallas kernels: 46.1 us -> 44.2 us
  local copies, waits for them, and re-layouts: 1.27 us -> 0.67 us
    pallas_call x1, Pallas kernels: 46.1 us -> 44.2 us  [local(): pl.pallas_call(kernel, out_shape=field, in_specs=[hbm] * 9, out_specs=vme...]
    unnamed x2 -> x0, local copies, waits for them, and re-layouts: 1.27 us -> none
    squeeze x0 -> x1, local copies, waits for them, and re-layouts: none -> 0.67 us  [local(): return (both[0], both[1])]
where the time goes in v3:
time: 45.6 us; the launch traced here: 45.5 us
  Pallas kernels  44.2 us (97%)
  local copies, waits for them, and re-layouts  0.67 us (1%)
  between operations  0.64 us (1%)
    pallas_call x1, Pallas kernels, local(): pl.pallas_call(kernel, out_shape=field, in_specs=[hbm] * 9, out_specs=vme...  44.2 us

profile of v3, /device:TPU:1, one launch (start us, length us, event | category | flops | bytes accessed | tf_op | source)
XLA Modules:
  0.0 45.5 jit_solution(14682792412188499593)
XLA Ops:
  0.6 44.2 %smooth.1 = f32[2,5,16,256]{3,2,1,0:T(8,128)S(1)} custom-call(f32[5,16,256]{2,1,0:T(8,128)} %psi_hbm.1, f32[5,16,256]{2,1,0:T(8,128)} %objective_hbm.1, s32[1,64]{1,0:T(1,128)} %bitcast.9, s32[1,512]{1,0:T(1,128)} %bitcast.7, s32[1,512]{1,0:T(1,128)} %bitcast.8, f32[16,512]{1,0:T(8,128)} %weight_hbm.1, bf16[5,5,5,16,256]{4,3,2,1,0:T(8,128)(2,1)} %stencil_hbm.1, ...), custom_call_target="tpu_custom_call" | custom-call | flops 20000000 | bytes 4000000 | tf_op jit(solution)/shard_map/smooth/pallas_call | solution.py:359
  44.9 0.7 %slice_bitcast_fusion = (f32[5,16,256]{2,1,0:T(8,128)}, f32[5,16,256]{2,1,0:T(8,128)}) fusion(f32[2,5,16,256]{3,2,1,0:T(8,128)S(1)} %smooth.1), kind=kLoop, calls=%fused_computation | loop fusion | bytes 327680 | tf_op jit(solution)/shard_map/squeeze | solution.py:406

commit v4 on v3

--- a/solution.py
+++ b/solution.py
@@ -309,7 +309,7 @@
         for i in range(NV):
             edge[0, i : i + 1, :] = lowered[i][NP - 1 : NP, :]
             edge[1, i : i + 1, :] = raised[i][0:1, :]
-        for k in range(1, ND):
+        for k in (1, 7, 2, 6, 3, 5, 4):
             send(remote(edge, edge, ls.at[it, k], lr.at[it, me], l_peer[k]))
         for k in range(1, ND):
             other = lax.rem(me + k, ND)

time: 45.6 us -> 45.1 us (0.989)
  Pallas kernels: 44.2 us -> 43.7 us
    pallas_call x1, Pallas kernels: 44.2 us -> 43.7 us  [local(): pl.pallas_call(kernel, out_shape=field, in_specs=[hbm] * 9, out_specs=vme...]
where the time goes in v4:
time: 45.1 us; the launch traced here: 45 us
  Pallas kernels  43.7 us (97%)
  local copies, waits for them, and re-layouts  0.67 us (1%)
  between operations  0.64 us (1%)
    pallas_call x1, Pallas kernels, local(): pl.pallas_call(kernel, out_shape=field, in_specs=[hbm] * 9, out_specs=vme...  43.7 us

profile of v4, /device:TPU:1, one launch (start us, length us, event | category | flops | bytes accessed | tf_op | source)
XLA Modules:
  0.0 45.0 jit_solution(5712955354515251122)
XLA Ops:
  0.6 43.7 %smooth.1 = f32[2,5,16,256]{3,2,1,0:T(8,128)S(1)} custom-call(f32[5,16,256]{2,1,0:T(8,128)} %psi_hbm.1, f32[5,16,256]{2,1,0:T(8,128)} %objective_hbm.1, s32[1,64]{1,0:T(1,128)} %bitcast.9, s32[1,512]{1,0:T(1,128)} %bitcast.7, s32[1,512]{1,0:T(1,128)} %bitcast.8, f32[16,512]{1,0:T(8,128)} %weight_hbm.1, bf16[5,5,5,16,256]{4,3,2,1,0:T(8,128)(2,1)} %stencil_hbm.1, ...), custom_call_target="tpu_custom_call" | custom-call | flops 20000000 | bytes 4000000 | tf_op jit(solution)/shard_map/smooth/pallas_call | solution.py:359
  44.3 0.7 %slice_bitcast_fusion = (f32[5,16,256]{2,1,0:T(8,128)}, f32[5,16,256]{2,1,0:T(8,128)}) fusion(f32[2,5,16,256]{3,2,1,0:T(8,128)S(1)} %smooth.1), kind=kLoop, calls=%fused_computation | loop fusion | bytes 327680 | tf_op jit(solution)/shard_map/squeeze | solution.py:406

commit v5 on v4

--- a/solution.py
+++ b/solution.py
@@ -235,7 +235,7 @@
             mine[j, i : i + 1, :] = low_all[i, j, NP - 1 : NP, :]
             mine[5 + j, i : i + 1, :] = up_all[i, j, 0:1, :]
             mine[10 + j, i : i + 1, :] = up_low[i, j, 0:1, :]
-    for k in range(1, ND):
+    for k in (1, 7, 2, 6, 3, 5, 4):
         send(remote(mine, mine, ms.at[k], mr.at[me], l_peer[k]))
 
     for it in range(ITERS):
@@ -343,7 +343,7 @@
             following = gathered(adjoint[...])
             zsend[1] = following
             zrecv[1, 0] = following
-            for k in (4, 3, 5, 2, 6, 1, 7):
+            for k in (3, 4, 5, 2, 6, 1, 7):
                 send(remote(zsend.at[1], zrecv.at[1, k], zs.at[1, k], zr.at[1, k], z_peer[k]))
 
     for copy in pending:

time: 45.1 us -> 45.1 us (level)
  no operation moved by 1% of the time
where the time goes in v5:
time: 45.1 us; the launch traced here: 45 us
  Pallas kernels  43.7 us (97%)
  local copies, waits for them, and re-layouts  0.67 us (1%)
  between operations  0.64 us (1%)
    pallas_call x1, Pallas kernels, local(): pl.pallas_call(kernel, out_shape=field, in_specs=[hbm] * 9, out_specs=vme...  43.7 us

profile of v5, /device:TPU:1, one launch (start us, length us, event | category | flops | bytes accessed | tf_op | source)
XLA Modules:
  0.0 45.0 jit_solution(14773155167862729459)
XLA Ops:
  0.6 43.7 %smooth.1 = f32[2,5,16,256]{3,2,1,0:T(8,128)S(1)} custom-call(f32[5,16,256]{2,1,0:T(8,128)} %psi_hbm.1, f32[5,16,256]{2,1,0:T(8,128)} %objective_hbm.1, s32[1,64]{1,0:T(1,128)} %bitcast.9, s32[1,512]{1,0:T(1,128)} %bitcast.7, s32[1,512]{1,0:T(1,128)} %bitcast.8, f32[16,512]{1,0:T(8,128)} %weight_hbm.1, bf16[5,5,5,16,256]{4,3,2,1,0:T(8,128)(2,1)} %stencil_hbm.1, ...), custom_call_target="tpu_custom_call" | custom-call | flops 20000000 | bytes 4000000 | tf_op jit(solution)/shard_map/smooth/pallas_call | solution.py:359
  44.3 0.7 %slice_bitcast_fusion = (f32[5,16,256]{2,1,0:T(8,128)}, f32[5,16,256]{2,1,0:T(8,128)}) fusion(f32[2,5,16,256]{3,2,1,0:T(8,128)S(1)} %smooth.1), kind=kLoop, calls=%fused_computation | loop fusion | bytes 327680 | tf_op jit(solution)/shard_map/squeeze | solution.py:406
